TPU v7x, 256 devices: a whole 4x4x8 slice. The times are simulated.
256 devices in a mesh: tis: 32 (over y_lo, z, core), ves: 8 (over y_hi, x).
Axes of the slice: x: 4, y: 4 (y_hi: 2, y_lo: 2; y = y_hi * 2 + y_lo), z: 8, core: 2. Of those that a mesh axis runs over, the one named last changes fastest.
Arguments:
- point_xyz: float32 [3, 131072], P(None, 'tis'), may hold values from 0 to 1
- point_cell: int32 [131072], P('tis'), may hold values from 0 to 127, never falling along the last dimension, each value on 1 to 4096 neighbouring positions
- seg_xyz: float32 [3, 32768], P(None, 'ves'), may hold values from 0 to 1
- seg_radius: float32 [32768], P('ves'), may hold values from 0.004 to 0.02
- conductance: float32 [32768], P('ves'), may hold values from 0.5 to 2
- flow_inv: float32 [32768], P('ves'), may hold values from 0.1 to 0.5
- parent: int32 [32768], P('ves'), may hold values from 0 to 32767, as said below
- inflow: float32 [8, 32768], P(None, 'ves'), may hold values from 2 to 4
- rate_table: float32 [8, 128], replicated, may hold values from 0.5 to 2
- half_sat: float32 [8], replicated, may hold values from 0.3 to 1
- diffusivity: float32 [8], replicated, may hold values from 0.5 to 2
- base_level: float32 [8], replicated, may hold values from -0.5 to 0.5
- sources: float32 [8, 32768], P(None, 'ves'), may hold values from 0.5 to 2
- contents: float32 [8, 32768], P(None, 'ves'), may hold values from 1 to 3
Outputs:
- tissue_level: float32 [8, 131072], P(None, 'tis')
- seg_sources: float32 [8, 32768], P(None, 'ves')
- blood_content: float32 [8, 32768], P(None, 'ves')
Inputs may be any that keep to these rules, and one draw needn't show every extreme that they name: Each segment is a root (parent equals its own index) or its parent lies among the 4096 segments before it: j - 4096 <= parent[j] < j. Points are ordered by region: point_cell never falls along the points.
All inputs are finite; a program needn't handle non-finite values.
Results may differ from a plain program's by a relative error of at most 0.0003.
Values sent between devices are 32-bit elements; how exact they have to be, the bound alone decides.
A program may use at most 128 MiB of HBM per device.

v0:
```python
import jax
import jax.numpy as jnp
from jax import lax
from jax.sharding import PartitionSpec as P

ITERS = 3


RELAX = 0.5
BALANCE = 0.5


def copy_for_each(x, axis):
    copies = jnp.broadcast_to(x, (lax.axis_size(axis), *x.shape))
    return lax.all_to_all(copies, axis, split_axis=0, concat_axis=0, tiled=True)


def taken_together(x, axis):
    return copy_for_each(x, axis).sum(axis=0)


def packed_total(arrays, axis):
    ravelled, at, gathered = (jnp.concatenate([a.reshape(-1) for a in arrays]), 0, [])
    so_far = taken_together(ravelled, axis)
    for a in arrays:
        gathered.append(so_far[at : at + a.size].reshape(a.shape))
        at += a.size
    return tuple(gathered)


def from_behind(value, axis, steps):
    count = lax.axis_size(axis)
    leading, last = (max(0, -steps), min(count, count - steps))
    return lax.ppermute(value, axis, [(source, source + steps) for source in range(leading, last)])


def split_up(x, dim, count):
    before, after = (x.shape[:dim], x.shape[dim + 1 :])
    return jnp.moveaxis(x.reshape(*before, count, -1, *after), dim, 0)


def sent_and_summed(x, axis, dim):
    pieces = split_up(x, dim, lax.axis_size(axis))
    arrived = lax.all_to_all(pieces, axis, split_axis=0, concat_axis=0, tiled=True)
    return arrived.sum(axis=0)


def padded_to(lines, count):
    spare = -lines.shape[0] % count
    if not spare:
        return lines
    return jnp.concatenate([lines, jnp.zeros((spare, *lines.shape[1:]), lines.dtype)])


def joined_along(pieces, dim):
    pieces = jnp.moveaxis(pieces, 0, dim)
    shape = pieces.shape
    return pieces.reshape(*shape[:dim], shape[dim] * shape[dim + 1], *shape[dim + 2 :])


def collect(x, axis, dim):
    pieces = copy_for_each(x, axis)
    return joined_along(pieces, dim)


def total_of(x, axes):
    own = sent_and_summed(padded_to(x, lax.axis_size(axes)), axes, 0)
    whole = collect(own, axes, 0)
    return whole[: len(x)].reshape(x.shape)


def together(arrays, axis):
    ravelled, at, gathered = (jnp.concatenate([a.reshape(-1) for a in arrays]), 0, [])
    so_far = total_of(ravelled, axis)
    for a in arrays:
        gathered.append(so_far[at : at + a.size].reshape(a.shape))
        at += a.size
    return tuple(gathered)


def kernel_rows(points, seg_pos, radius):
    dist_sq = (points[0][:, None] - seg_pos[0][None, :]) ** 2
    dist_sq = dist_sq + (points[1][:, None] - seg_pos[1][None, :]) ** 2
    dist_sq = dist_sq + (points[2][:, None] - seg_pos[2][None, :]) ** 2
    return lax.rsqrt(dist_sq + (radius * radius)[None, :]).astype(jnp.bfloat16)


def body(
    point_xyz,
    point_cell,
    seg_xyz,
    seg_radius,
    conductance,
    flow_inv,
    parent,
    inflow,
    rate_table,
    half_sat,
    diffusivity,
    base_level,
    sources,
    contents,
):
    pt_rows = point_xyz.shape[1]
    seg_cols = seg_xyz.shape[1]
    solutes = sources.shape[0]
    n_tis = lax.axis_size("tis")
    n_ves = lax.axis_size("ves")
    total_pts = pt_rows * n_tis
    total_segs = seg_cols * n_ves
    blk_rows = min(512, pt_rows)
    n_blocks = pt_rows // blk_rows
    n_cells = rate_table.shape[1]
    onehot = (point_cell[None, :] == jnp.arange(n_cells, dtype=jnp.int32)[:, None]).astype(
        jnp.float32
    )
    rates_pts = jnp.dot(
        rate_table, onehot, precision=lax.Precision.HIGHEST, preferred_element_type=jnp.float32
    )
    point_blocks = point_xyz.reshape(3, n_blocks, blk_rows).transpose(1, 0, 2)
    dims_rows = (((1,), (1,)), ((), ()))
    kernel_tiles = lax.map(
        lambda pts_block: kernel_rows(pts_block, seg_xyz, seg_radius), point_blocks
    ).reshape(pt_rows, seg_cols)
    ves_index = lax.axis_index("ves")
    global_seg = ves_index * seg_cols + jnp.arange(seg_cols, dtype=jnp.int32)
    is_root = parent == global_seg
    local_parent = jnp.where(is_root, global_seg, parent) - (ves_index * seg_cols - seg_cols)
    tissue_level = jnp.zeros((solutes, pt_rows), jnp.float32)
    for sweep in range(ITERS):
        src_bf = sources.astype(jnp.bfloat16)
        partial_value = lax.dot_general(
            src_bf, kernel_tiles, dims_rows, preferred_element_type=jnp.float32
        )
        summed, source_total = packed_total((partial_value, jnp.sum(sources, axis=1)), "ves")
        tissue_level = base_level[:, None] + summed / (diffusivity[:, None] * total_segs)
        sink_field = rates_pts * tissue_level / (jnp.abs(tissue_level) + half_sat[:, None])
        outflow = contents - sources * flow_inv[None, :]
        upstream = from_behind(outflow, "ves", 1)
        joined = jnp.concatenate([upstream, outflow], axis=1)
        fetched = jnp.take(joined, local_parent, axis=1)
        contents = jnp.where(is_root[None, :], inflow, fetched)
        wall_part = jnp.dot(
            sink_field.astype(jnp.bfloat16), kernel_tiles, preferred_element_type=jnp.float32
        )
        sink_local = jnp.sum(sink_field, axis=1)
        wall_raw, sink_total = together((wall_part, sink_local), "tis")
        wall_field = wall_raw / (diffusivity[:, None] * total_pts)
        sources = RELAX * sources + RELAX * conductance[None, :] * (contents - wall_field)
        base_level = base_level + BALANCE * (source_total / total_segs - sink_total / total_pts)
    return (tissue_level, sources, contents)


def solution(mesh):
    return jax.shard_map(
        body,
        mesh=mesh,
        in_specs=(
            P(None, "tis"),
            P("tis"),
            P(None, "ves"),
            P("ves"),
            P("ves"),
            P("ves"),
            P("ves"),
            P(None, "ves"),
            P(),
            P(),
            P(),
            P(),
            P(None, "ves"),
            P(None, "ves"),
        ),
        out_specs=(P(None, "tis"), P(None, "ves"), P(None, "ves")),
        check_vma=False,
    )
```

profile of v0, /device:TPU:1, one launch (start us, length us, event | category | flops | bytes accessed | tf_op | source)
XLA Modules:
  0.0 341.0 jit_solution(15811689487358662564)
XLA Ops:
  1.5 52.6 %while.12 = (s32[]{:T(128)}, bf16[8,512,4096]{2,1,0:T(8,128)(2,1)}, f32[8,3,512]{2,1,0:T(4,128)}, f32[3,4096]{1,0:T(4,128)}, f32[1,4096]{1,0:T(1,128)S(1)}, /*index=5*/s32[]{:T(128)}, s32[]{:T(128)}, s32[]{}, s32[]{}) while((s32[]{:T(128)}, bf16[8,512,4096]{2,1,0:T(8,128)(2,1)}, f32[8,3,512]{2,1,0:T(4,128)}, f32[3,4096]{1,0:T(4,128)}, ...), condition=%wide.region_1.2_spmd, body=%wide.region_0.1_spmd.sunk | while | flops 20971524 | bytes 4377217 | solution.py:122
  2.3 1.0 fusion.29
  3.3 4.7 %fusion.30 = bf16[8,512,4096]{2,1,0:T(8,128)(2,1)} fusion(bf16[8,512,4096]{2,1,0:T(8,128)(2,1)} %get-tuple-element.178, s32[]{:T(128)} %get-tuple-element.177, f32[4096]{0:T(1024)S(1)} %bitcast.84, f32[4096]{0:T(1024)S(1)} %bitcast.81, f32[512]{0:T(512)S(1)} %bitcast.93, f32[4096]{0:T(1024)S(1)} %bitcast.82, f32[512]{0:T(512)S(1)} %bitcast.92, ...), kind=kLoop, calls=%fused_computation.4.clone.1 | loop fusion | flops 20971520 | bytes 4266496 | tf_op jit(solution)/shard_map/while/body/jit(dynamic_update_index_in_dim)/dynamic_update_slice | solution.py:122
  8.8 1.0 fusion.29
  9.8 4.8 %fusion.30 = bf16[8,512,4096]{2,1,0:T(8,128)(2,1)} fusion(bf16[8,512,4096]{2,1,0:T(8,128)(2,1)} %get-tuple-element.178, s32[]{:T(128)} %get-tuple-element.177, f32[4096]{0:T(1024)S(1)} %bitcast.84, f32[4096]{0:T(1024)S(1)} %bitcast.81, f32[512]{0:T(512)S(1)} %bitcast.93, f32[4096]{0:T(1024)S(1)} %bitcast.82, f32[512]{0:T(512)S(1)} %bitcast.92, ...), kind=kLoop, calls=%fused_computation.4.clone.1 | loop fusion | flops 20971520 | bytes 4266496 | tf_op jit(solution)/shard_map/while/body/jit(dynamic_update_index_in_dim)/dynamic_update_slice | solution.py:122
  15.4 1.0 fusion.29
  16.4 4.8 %fusion.30 = bf16[8,512,4096]{2,1,0:T(8,128)(2,1)} fusion(bf16[8,512,4096]{2,1,0:T(8,128)(2,1)} %get-tuple-element.178, s32[]{:T(128)} %get-tuple-element.177, f32[4096]{0:T(1024)S(1)} %bitcast.84, f32[4096]{0:T(1024)S(1)} %bitcast.81, f32[512]{0:T(512)S(1)} %bitcast.93, f32[4096]{0:T(1024)S(1)} %bitcast.82, f32[512]{0:T(512)S(1)} %bitcast.92, ...), kind=kLoop, calls=%fused_computation.4.clone.1 | loop fusion | flops 20971520 | bytes 4266496 | tf_op jit(solution)/shard_map/while/body/jit(dynamic_update_index_in_dim)/dynamic_update_slice | solution.py:122
  22.0 1.0 fusion.29
  23.0 4.8 %fusion.30 = bf16[8,512,4096]{2,1,0:T(8,128)(2,1)} fusion(bf16[8,512,4096]{2,1,0:T(8,128)(2,1)} %get-tuple-element.178, s32[]{:T(128)} %get-tuple-element.177, f32[4096]{0:T(1024)S(1)} %bitcast.84, f32[4096]{0:T(1024)S(1)} %bitcast.81, f32[512]{0:T(512)S(1)} %bitcast.93, f32[4096]{0:T(1024)S(1)} %bitcast.82, f32[512]{0:T(512)S(1)} %bitcast.92, ...), kind=kLoop, calls=%fused_computation.4.clone.1 | loop fusion | flops 20971520 | bytes 4266496 | tf_op jit(solution)/shard_map/while/body/jit(dynamic_update_index_in_dim)/dynamic_update_slice | solution.py:122
  28.6 1.0 fusion.29
  29.6 4.7 %fusion.30 = bf16[8,512,4096]{2,1,0:T(8,128)(2,1)} fusion(bf16[8,512,4096]{2,1,0:T(8,128)(2,1)} %get-tuple-element.178, s32[]{:T(128)} %get-tuple-element.177, f32[4096]{0:T(1024)S(1)} %bitcast.84, f32[4096]{0:T(1024)S(1)} %bitcast.81, f32[512]{0:T(512)S(1)} %bitcast.93, f32[4096]{0:T(1024)S(1)} %bitcast.82, f32[512]{0:T(512)S(1)} %bitcast.92, ...), kind=kLoop, calls=%fused_computation.4.clone.1 | loop fusion | flops 20971520 | bytes 4266496 | tf_op jit(solution)/shard_map/while/body/jit(dynamic_update_index_in_dim)/dynamic_update_slice | solution.py:122
  35.1 1.0 fusion.29
  36.2 4.8 %fusion.30 = bf16[8,512,4096]{2,1,0:T(8,128)(2,1)} fusion(bf16[8,512,4096]{2,1,0:T(8,128)(2,1)} %get-tuple-element.178, s32[]{:T(128)} %get-tuple-element.177, f32[4096]{0:T(1024)S(1)} %bitcast.84, f32[4096]{0:T(1024)S(1)} %bitcast.81, f32[512]{0:T(512)S(1)} %bitcast.93, f32[4096]{0:T(1024)S(1)} %bitcast.82, f32[512]{0:T(512)S(1)} %bitcast.92, ...), kind=kLoop, calls=%fused_computation.4.clone.1 | loop fusion | flops 20971520 | bytes 4266496 | tf_op jit(solution)/shard_map/while/body/jit(dynamic_update_index_in_dim)/dynamic_update_slice | solution.py:122
  42.7 4.7 %fusion.30 = bf16[8,512,4096]{2,1,0:T(8,128)(2,1)} fusion(bf16[8,512,4096]{2,1,0:T(8,128)(2,1)} %get-tuple-element.178, s32[]{:T(128)} %get-tuple-element.177, f32[4096]{0:T(1024)S(1)} %bitcast.84, f32[4096]{0:T(1024)S(1)} %bitcast.81, f32[512]{0:T(512)S(1)} %bitcast.93, f32[4096]{0:T(1024)S(1)} %bitcast.82, f32[512]{0:T(512)S(1)} %bitcast.92, ...), kind=kLoop, calls=%fused_computation.4.clone.1 | loop fusion | flops 20971520 | bytes 4266496 | tf_op jit(solution)/shard_map/while/body/jit(dynamic_update_index_in_dim)/dynamic_update_slice | solution.py:122
  49.3 4.8 %fusion.30 = bf16[8,512,4096]{2,1,0:T(8,128)(2,1)} fusion(bf16[8,512,4096]{2,1,0:T(8,128)(2,1)} %get-tuple-element.178, s32[]{:T(128)} %get-tuple-element.177, f32[4096]{0:T(1024)S(1)} %bitcast.84, f32[4096]{0:T(1024)S(1)} %bitcast.81, f32[512]{0:T(512)S(1)} %bitcast.93, f32[4096]{0:T(1024)S(1)} %bitcast.82, f32[512]{0:T(512)S(1)} %bitcast.92, ...), kind=kLoop, calls=%fused_computation.4.clone.1 | loop fusion | flops 20971520 | bytes 4266496 | tf_op jit(solution)/shard_map/while/body/jit(dynamic_update_index_in_dim)/dynamic_update_slice | solution.py:122
  54.1 15.1 %convolution_bitcast_fusion.6 = f32[1,32,8,128]{3,2,1,0:T(8,128)S(1)} fusion(bf16[4096,4096]{1,0:T(8,128)(2,1)} %bitcast.74, f32[8,4096]{1,0:T(8,128)S(1)} %copy-done.2), kind=kOutput, calls=%fused_computation.15 | convolution fusion | flops 268468224 | bytes 33816576 | tf_op jit(solution)/shard_map/dot_general | solution.py:132
  69.4 1.5 broadcast_in_dim.41
  70.9 7.5 %all-to-all-start = ((f32[8,1,32776]{2,1,0:T(1,128)}), f32[8,1,32776]{2,1,0:T(1,128)S(1)}, u32[]{:S(2)}, u32[]{:S(2)}) async-start(f32[8,1,32776]{2,1,0:T(1,128)} %broadcast_in_dim.41), calls=%async_computation | async-start | bytes 2105344 | tf_op jit(solution)/shard_map/all_to_all | solution.py:15
  78.4 3.4 collective-permute-start
  81.8 13.9 %all-to-all-done = f32[8,1,32776]{2,1,0:T(1,128)S(1)} async-done(((f32[8,1,32776]{2,1,0:T(1,128)}), f32[8,1,32776]{2,1,0:T(1,128)S(1)}, u32[]{:S(2)}, u32[]{:S(2)}) %all-to-all-start) | async-done | bytes 1048864 | tf_op jit(solution)/shard_map/all_to_all | solution.py:15
  97.5 12.8 %convolution_bitcast_fusion.5 = f32[1,32,8,128]{3,2,1,0:T(8,128)S(1)} fusion(bf16[4096,4096]{1,0:T(8,128)(2,1)} %bitcast.75, bf16[8,4096]{1,0:T(8,128)(2,1)S(1)} %get-tuple-element.103), kind=kOutput, calls=%fused_computation.14 | convolution fusion | flops 268435456 | bytes 33751040 | tf_op jit(solution)/shard_map/dot_general | solution.py:143
  111.4 9.6 %all-to-all-start.1 = ((f32[32,1,1025]{2,1,0:T(1,128)}), f32[32,1,1025]{2,1,0:T(1,128)S(1)}, u32[]{:S(2)}, u32[]{:S(2)}) async-start(f32[32,1,1025]{2,1,0:T(1,128)} %all_to_all.43), calls=%async_computation.1 | async-start | bytes 294912 | tf_op jit(solution)/shard_map/all_to_all | solution.py:44
  121.0 9.2 %all-to-all-done.1 = f32[32,1,1025]{2,1,0:T(1,128)S(1)} async-done(((f32[32,1,1025]{2,1,0:T(1,128)}), f32[32,1,1025]{2,1,0:T(1,128)S(1)}, u32[]{:S(2)}, u32[]{:S(2)}) %all-to-all-start.1) | async-done | bytes 131232 | tf_op jit(solution)/shard_map/all_to_all | solution.py:44
  131.1 5.2 %all-to-all-start.2 = ((f32[32,1,1025]{2,1,0:T(1,128)}), f32[32,1,1025]{2,1,0:T(1,128)S(1)}, u32[]{:S(2)}, u32[]{:S(2)}) async-start(f32[32,1,1025]{2,1,0:T(1,128)} %broadcast_in_dim.42), calls=%async_computation.2 | async-start | bytes 294912 | tf_op jit(solution)/shard_map/all_to_all | solution.py:15
  136.4 2.7 copy.108
  139.1 12.9 %gather_fusion = f32[4096,8]{1,0:T(8,128)S(1)} fusion(f32[8,8192]{0,1:T(8,128)} %copy.108, s32[4096]{0:T(1024)S(1)} %fusion.9), kind=kCustom, calls=%fused_computation.clone | custom fusion | bytes 278528 | tf_op jit(solution)/shard_map/jit(_take)/gather | solution.py:141
  153.3 14.5 %convolution_bitcast_fusion.4 = f32[1,32,8,128]{3,2,1,0:T(8,128)S(1)} fusion(bf16[4096,4096]{1,0:T(8,128)(2,1)} %bitcast.76, f32[8,4096]{1,0:T(8,128)S(1)} %get-tuple-element.99), kind=kOutput, calls=%fused_computation.13 | convolution fusion | flops 268468224 | bytes 33816576 | tf_op jit(solution)/shard_map/dot_general | solution.py:132
  168.0 1.5 broadcast_in_dim.44
  169.6 3.9 %all-to-all-start.3 = ((f32[8,1,32776]{2,1,0:T(1,128)}), f32[8,1,32776]{2,1,0:T(1,128)S(1)}, u32[]{:S(2)}, u32[]{:S(2)}) async-start(f32[8,1,32776]{2,1,0:T(1,128)} %broadcast_in_dim.44), calls=%async_computation.3 | async-start | bytes 2105344 | tf_op jit(solution)/shard_map/all_to_all | solution.py:15
  173.5 17.4 %all-to-all-done.3 = f32[8,1,32776]{2,1,0:T(1,128)S(1)} async-done(((f32[8,1,32776]{2,1,0:T(1,128)}), f32[8,1,32776]{2,1,0:T(1,128)S(1)}, u32[]{:S(2)}, u32[]{:S(2)}) %all-to-all-start.3) | async-done | bytes 1048864 | tf_op jit(solution)/shard_map/all_to_all | solution.py:15
  191.9 12.8 %convolution_bitcast_fusion.3 = f32[1,32,8,128]{3,2,1,0:T(8,128)S(1)} fusion(bf16[4096,4096]{1,0:T(8,128)(2,1)} %bitcast.77, bf16[8,4096]{1,0:T(8,128)(2,1)S(1)} %get-tuple-element.101), kind=kOutput, calls=%fused_computation.12 | convolution fusion | flops 268435456 | bytes 33751040 | tf_op jit(solution)/shard_map/dot_general | solution.py:143
  205.8 8.5 %all-to-all-start.4 = ((f32[32,1,1025]{2,1,0:T(1,128)}), f32[32,1,1025]{2,1,0:T(1,128)S(1)}, u32[]{:S(2)}, u32[]{:S(2)}) async-start(f32[32,1,1025]{2,1,0:T(1,128)} %all_to_all.47), calls=%async_computation.4 | async-start | bytes 294912 | tf_op jit(solution)/shard_map/all_to_all | solution.py:44
  214.2 2.5 collective-permute-start.1
  216.7 7.1 %all-to-all-done.4 = f32[32,1,1025]{2,1,0:T(1,128)S(1)} async-done(((f32[32,1,1025]{2,1,0:T(1,128)}), f32[32,1,1025]{2,1,0:T(1,128)S(1)}, u32[]{:S(2)}, u32[]{:S(2)}) %all-to-all-start.4) | async-done | bytes 131232 | tf_op jit(solution)/shard_map/all_to_all | solution.py:44
  224.7 4.9 %all-to-all-start.5 = ((f32[32,1,1025]{2,1,0:T(1,128)}), f32[32,1,1025]{2,1,0:T(1,128)S(1)}, u32[]{:S(2)}, u32[]{:S(2)}) async-start(f32[32,1,1025]{2,1,0:T(1,128)} %broadcast_in_dim.45), calls=%async_computation.5 | async-start | bytes 294912 | tf_op jit(solution)/shard_map/all_to_all | solution.py:15
  229.7 2.7 copy.112
  232.4 12.9 %gather_fusion.1 = f32[4096,8]{1,0:T(8,128)S(1)} fusion(f32[8,8192]{0,1:T(8,128)} %copy.112, s32[4096]{0:T(1024)S(1)} %fusion.9), kind=kCustom, calls=%fused_computation.1.clone | custom fusion | bytes 278528 | tf_op jit(solution)/shard_map/jit(_take)/gather | solution.py:141
  246.6 14.5 %convolution_bitcast_fusion.2 = f32[1,32,8,128]{3,2,1,0:T(8,128)S(1)} fusion(bf16[4096,4096]{1,0:T(8,128)(2,1)} %bitcast.78, f32[8,4096]{1,0:T(8,128)S(1)} %get-tuple-element.97), kind=kOutput, calls=%fused_computation.11 | convolution fusion | flops 268468224 | bytes 33816576 | tf_op jit(solution)/shard_map/dot_general | solution.py:132
  261.3 1.5 broadcast_in_dim.76
  262.8 3.6 %all-to-all-start.6 = ((f32[8,1,32776]{2,1,0:T(1,128)}), f32[8,1,32776]{2,1,0:T(1,128)S(1)}, u32[]{:S(2)}, u32[]{:S(2)}) async-start(f32[8,1,32776]{2,1,0:T(1,128)} %broadcast_in_dim.76), calls=%async_computation.6 | async-start | bytes 2105344 | tf_op jit(solution)/shard_map/all_to_all | solution.py:15
  266.4 17.3 %all-to-all-done.6 = f32[8,1,32776]{2,1,0:T(1,128)S(1)} async-done(((f32[8,1,32776]{2,1,0:T(1,128)}), f32[8,1,32776]{2,1,0:T(1,128)S(1)}, u32[]{:S(2)}, u32[]{:S(2)}) %all-to-all-start.6) | async-done | bytes 1048864 | tf_op jit(solution)/shard_map/all_to_all | solution.py:15
  285.4 12.8 %convolution_bitcast_fusion.1 = f32[1,32,8,128]{3,2,1,0:T(8,128)S(1)} fusion(bf16[4096,4096]{1,0:T(8,128)(2,1)} %bitcast.79, bf16[8,4096]{1,0:T(8,128)(2,1)S(1)} %get-tuple-element.94), kind=kOutput, calls=%fused_computation.10 | convolution fusion | flops 268435456 | bytes 33751040 | tf_op jit(solution)/shard_map/dot_general | solution.py:143
  299.3 8.8 %all-to-all-start.7 = ((f32[32,1,1025]{2,1,0:T(1,128)}), f32[32,1,1025]{2,1,0:T(1,128)S(1)}, u32[]{:S(2)}, u32[]{:S(2)}) async-start(f32[32,1,1025]{2,1,0:T(1,128)} %all_to_all.51), calls=%async_computation.7 | async-start | bytes 294912 | tf_op jit(solution)/shard_map/all_to_all | solution.py:44
  308.1 2.5 collective-permute-start.2
  310.6 7.1 %all-to-all-done.7 = f32[32,1,1025]{2,1,0:T(1,128)S(1)} async-done(((f32[32,1,1025]{2,1,0:T(1,128)}), f32[32,1,1025]{2,1,0:T(1,128)S(1)}, u32[]{:S(2)}, u32[]{:S(2)}) %all-to-all-start.7) | async-done | bytes 131232 | tf_op jit(solution)/shard_map/all_to_all | solution.py:44
  318.6 4.9 %all-to-all-start.8 = ((f32[32,1,1025]{2,1,0:T(1,128)}), f32[32,1,1025]{2,1,0:T(1,128)S(1)}, u32[]{:S(2)}, u32[]{:S(2)}) async-start(f32[32,1,1025]{2,1,0:T(1,128)} %broadcast_in_dim.77), calls=%async_computation.8 | async-start | bytes 294912 | tf_op jit(solution)/shard_map/all_to_all | solution.py:15
  323.5 2.6 copy.115
  326.1 12.9 %gather_fusion.2 = f32[4096,8]{1,0:T(8,128)S(1)} fusion(f32[8,8192]{0,1:T(8,128)} %copy.115, s32[4096]{0:T(1024)S(1)} %fusion.9), kind=kCustom, calls=%fused_computation.2.clone | custom fusion | bytes 278528 | tf_op jit(solution)/shard_map/jit(_take)/gather | solution.py:141
  (106 shorter events, 24.3 us)
Async XLA Ops:
  0.6 96.0 %copy-start = (f32[8,128]{1,0:T(8,128)S(1)}, f32[8,128]{1,0:T(8,128)}, u32[]{:S(2)}) copy-start(f32[8,128]{1,0:T(8,128)} %param.26) | copy-start | bytes 12292
  1.5 52.6 %copy-start.2 = (f32[8,4096]{1,0:T(8,128)S(1)}, f32[8,4096]{1,0:T(8,128)}, u32[]{:S(2)}) copy-start(f32[8,4096]{1,0:T(8,128)} %param.30) | copy-start | bytes 393220
  54.1 15.2 %copy-start.4 = (f32[4096]{0:T(1024)S(1)}, f32[4096]{0:T(1024)}, u32[]{:S(2)}) copy-start(f32[4096]{0:T(1024)} %param.23) | copy-start | bytes 49156
  54.1 15.2 %copy-start.5 = (f32[8,4096]{1,0:T(8,128)S(1)}, f32[8,4096]{1,0:T(8,128)}, u32[]{:S(2)}) copy-start(f32[8,4096]{1,0:T(8,128)} %param.31) | copy-start | bytes 393220
  54.1 27.7 %copy-start.11 = (f32[8]{0:T(128)S(1)}, f32[8]{0:T(128)}, u32[]{:S(2)}) copy-start(f32[8]{0:T(128)} %param.28) | copy-start | bytes 100
  54.1 27.7 %copy-start.7 = (f32[4096]{0:T(1024)S(1)}, f32[4096]{0:T(1024)}, u32[]{:S(2)}) copy-start(f32[4096]{0:T(1024)} %param.22) | copy-start | bytes 49156
  54.1 42.5 %copy-start.8 = (f32[8]{0:T(128)S(1)}, f32[8]{0:T(128)}, u32[]{:S(2)}) copy-start(f32[8]{0:T(128)} %param.27) | copy-start | bytes 100
  54.1 42.5 %copy-start.9 = (f32[8]{0:T(128)S(1)}, f32[8]{0:T(128)}, u32[]{:S(2)}) copy-start(f32[8]{0:T(128)} %param.29) | copy-start | bytes 100
  54.1 42.5 %copy-start.10 = (s32[4096]{0:T(1024)S(1)}, s32[4096]{0:T(1024)}, u32[]{:S(2)}) copy-start(s32[4096]{0:T(1024)} %param.19) | copy-start | bytes 49156
  70.9 24.8 %all-to-all-start = ((f32[8,1,32776]{2,1,0:T(1,128)}), f32[8,1,32776]{2,1,0:T(1,128)S(1)}, u32[]{:S(2)}, u32[]{:S(2)}) async-start(f32[8,1,32776]{2,1,0:T(1,128)} %broadcast_in_dim.41), calls=%async_computation | async-start | bytes 2105344 | tf_op jit(solution)/shard_map/all_to_all | solution.py:15
  78.4 57.9 %collective-permute-start = (f32[8,4096]{1,0:T(8,128)S(1)}, f32[8,4096]{1,0:T(8,128)S(1)}, u32[]{:S(2)}, u32[]{:S(2)}) collective-permute-start(f32[8,4096]{1,0:T(8,128)S(1)} %get-tuple-element.111), channel_id=1, source_target_pairs={{0,1},{1,2},{2,3},{3,4},{4,5},{5,6},{6,7},{8,9},{9,10},{10,11},{11... | collective-permute-start | bytes 393224 | tf_op jit(solution)/shard_map/ppermute | solution.py:34
  97.5 23.5 %copy-start.6 = (s32[4096]{0:T(1024)S(1)}, s32[4096]{0:T(1024)}, u32[]{:S(2)}) copy-start(s32[4096]{0:T(1024)} %param.24) | copy-start | bytes 49156
  110.3 42.8 %copy-start.3 = (f32[8,4096]{1,0:T(8,128)S(1)}, f32[8,4096]{1,0:T(8,128)}, u32[]{:S(2)}) copy-start(f32[8,4096]{1,0:T(8,128)} %param.25) | copy-start | bytes 393220
  111.4 18.9 %all-to-all-start.1 = ((f32[32,1,1025]{2,1,0:T(1,128)}), f32[32,1,1025]{2,1,0:T(1,128)S(1)}, u32[]{:S(2)}, u32[]{:S(2)}) async-start(f32[32,1,1025]{2,1,0:T(1,128)} %all_to_all.43), calls=%async_computation.1 | async-start | bytes 294912 | tf_op jit(solution)/shard_map/all_to_all | solution.py:44
  131.1 21.5 %all-to-all-start.2 = ((f32[32,1,1025]{2,1,0:T(1,128)}), f32[32,1,1025]{2,1,0:T(1,128)S(1)}, u32[]{:S(2)}, u32[]{:S(2)}) async-start(f32[32,1,1025]{2,1,0:T(1,128)} %broadcast_in_dim.42), calls=%async_computation.2 | async-start | bytes 294912 | tf_op jit(solution)/shard_map/all_to_all | solution.py:15
  169.6 21.3 %all-to-all-start.3 = ((f32[8,1,32776]{2,1,0:T(1,128)}), f32[8,1,32776]{2,1,0:T(1,128)S(1)}, u32[]{:S(2)}, u32[]{:S(2)}) async-start(f32[8,1,32776]{2,1,0:T(1,128)} %broadcast_in_dim.44), calls=%async_computation.3 | async-start | bytes 2105344 | tf_op jit(solution)/shard_map/all_to_all | solution.py:15
  205.8 18.1 %all-to-all-start.4 = ((f32[32,1,1025]{2,1,0:T(1,128)}), f32[32,1,1025]{2,1,0:T(1,128)S(1)}, u32[]{:S(2)}, u32[]{:S(2)}) async-start(f32[32,1,1025]{2,1,0:T(1,128)} %all_to_all.47), calls=%async_computation.4 | async-start | bytes 294912 | tf_op jit(solution)/shard_map/all_to_all | solution.py:44
  214.2 15.4 %collective-permute-start.1 = (f32[8,4096]{1,0:T(8,128)S(1)}, f32[8,4096]{1,0:T(8,128)S(1)}, u32[]{:S(2)}, u32[]{:S(2)}) collective-permute-start(f32[8,4096]{1,0:T(8,128)S(1)} %get-tuple-element.98), channel_id=1, source_target_pairs={{0,1},{1,2},{2,3},{3,4},{4,5},{5,6},{6,7},{8,9},{9,10},{10,11},{11... | collective-permute-start | bytes 393224 | tf_op jit(solution)/shard_map/ppermute | solution.py:34
  224.7 21.2 %all-to-all-start.5 = ((f32[32,1,1025]{2,1,0:T(1,128)}), f32[32,1,1025]{2,1,0:T(1,128)S(1)}, u32[]{:S(2)}, u32[]{:S(2)}) async-start(f32[32,1,1025]{2,1,0:T(1,128)} %broadcast_in_dim.45), calls=%async_computation.5 | async-start | bytes 294912 | tf_op jit(solution)/shard_map/all_to_all | solution.py:15
  262.8 20.9 %all-to-all-start.6 = ((f32[8,1,32776]{2,1,0:T(1,128)}), f32[8,1,32776]{2,1,0:T(1,128)S(1)}, u32[]{:S(2)}, u32[]{:S(2)}) async-start(f32[8,1,32776]{2,1,0:T(1,128)} %broadcast_in_dim.76), calls=%async_computation.6 | async-start | bytes 2105344 | tf_op jit(solution)/shard_map/all_to_all | solution.py:15
  285.4 55.6 %copy-start.1 = (f32[8,128]{1,0:T(8,128)S(1)}, f32[8,128]{1,0:T(8,128)}, u32[]{:S(2)}) copy-start(f32[8,128]{1,0:T(8,128)} %param.26) | copy-start | bytes 12292
  299.3 18.5 %all-to-all-start.7 = ((f32[32,1,1025]{2,1,0:T(1,128)}), f32[32,1,1025]{2,1,0:T(1,128)S(1)}, u32[]{:S(2)}, u32[]{:S(2)}) async-start(f32[32,1,1025]{2,1,0:T(1,128)} %all_to_all.51), calls=%async_computation.7 | async-start | bytes 294912 | tf_op jit(solution)/shard_map/all_to_all | solution.py:44
  308.1 15.4 %collective-permute-start.2 = (f32[8,4096]{1,0:T(8,128)S(1)}, f32[8,4096]{1,0:T(8,128)S(1)}, u32[]{:S(2)}, u32[]{:S(2)}) collective-permute-start(f32[8,4096]{1,0:T(8,128)S(1)} %get-tuple-element.96), channel_id=1, source_target_pairs={{0,1},{1,2},{2,3},{3,4},{4,5},{5,6},{6,7},{8,9},{9,10},{10,11},{11... | collective-permute-start | bytes 393224 | tf_op jit(solution)/shard_map/ppermute | solution.py:34
  318.6 21.1 %all-to-all-start.8 = ((f32[32,1,1025]{2,1,0:T(1,128)}), f32[32,1,1025]{2,1,0:T(1,128)S(1)}, u32[]{:S(2)}, u32[]{:S(2)}) async-start(f32[32,1,1025]{2,1,0:T(1,128)} %broadcast_in_dim.77), calls=%async_computation.8 | async-start | bytes 294912 | tf_op jit(solution)/shard_map/all_to_all | solution.py:15
where the time goes:
time: 343 us; the launch traced here: 341 us
  matrix products  83.4 us (24%)
  local copies, waits for them, and re-layouts  73.6 us (21%)
  waiting for transfers between devices  72.2 us (21%)
  starting transfers between devices  65.2 us (19%)
  other arithmetic  45.3 us (13%)
    all_to_all x6, waiting for transfers between devices, copy_for_each(): return lax.all_to_all(copies, axis, split_axis=0, concat_axis=0, tiled=True)  48.7 us
    dot_general x3, matrix products, body(): lax.dot_general(src_bf, kernel_tiles, dims_rows, preferred_element_type=j...  44.1 us
    gather x6, local copies, waits for them, and re-layouts, body(): fetched = jnp.take(joined, local_parent, axis=1)  40.5 us
    dot_general x3, matrix products, body(): jnp.dot(sink_field.astype(jnp.bfloat16), kernel_tiles, preferred_element_...  38.5 us
    dynamic_update_slice x8, other arithmetic, body(): lax.map(lambda pts_block: kernel_rows(pts_block, seg_xyz, seg_radius), po...  38.1 us
    all_to_all x6, starting transfers between devices, copy_for_each(): return lax.all_to_all(copies, axis, split_axis=0, concat_axis=0, tiled=True)  30 us
    all_to_all x3, starting transfers between devices, sent_and_summed(): lax.all_to_all(pieces, axis, split_axis=0, concat_axis=0, tiled=True)  26.9 us
    all_to_all x3, waiting for transfers between devices, sent_and_summed(): lax.all_to_all(pieces, axis, split_axis=0, concat_axis=0, tiled=True)  23.5 us
  transfers between devices with their start and end apart: 12, of which 6 were waited for; matrix products, arithmetic and copies ran while one was open for 19% of the time, Pallas kernels for 0%

commit v1 on v0

v1 whole, which is shorter than its diff:
```python
import functools

import jax
import jax.numpy as jnp
from jax import lax
from jax.experimental import pallas as pl
from jax.experimental.pallas import tpu as pltpu
from jax.sharding import PartitionSpec as P

ITERS = 3
RELAX = 0.5
BALANCE = 0.5
LANES = 128
FEATURES = 128
MESH = pl.DeviceIdType.MESH


def pieces(x):
    high = x.astype(jnp.bfloat16).astype(jnp.float32)
    rest = x - high
    middle = rest.astype(jnp.bfloat16).astype(jnp.float32)
    return high, middle, (rest - middle).astype(jnp.bfloat16).astype(jnp.float32)


def dot(a, b):
    return jnp.dot(a, b, preferred_element_type=jnp.float32)


def dot_nt(a, b):
    return lax.dot_general(a, b, (((1,), (1,)), ((), ())), preferred_element_type=jnp.float32)


def at(i, size):
    return pl.ds(pl.multiple_of(i * size, size), size)


def kernel(
    n_ves,
    n_z,
    pts,
    segs,
    point_ref,
    cell_ref,
    seg_ref,
    radius_ref,
    cond_ref,
    flow_ref,
    parent_ref,
    inflow_ref,
    table_ref,
    half_ref,
    diff_ref,
    base_ref,
    sources_ref,
    contents_ref,
    level_out,
    sources_out,
    contents_out,
    tile,
    point_feat,
    seg_feat,
    feat,
    rates,
    base,
    t_sum,
    t_send,
    t_recv,
    level,
    sink,
    sink_sum,
    wall,
    a_send,
    a_recv,
    b_send,
    b_recv,
    src,
    cont,
    joined,
    t_ss,
    t_rs,
    l_ss,
    l_rs,
    a_ss,
    a_rs,
    b_ss,
    b_rs,
    z_ss,
    z_rs,
    c_ss,
    c_rs,
    o_ss,
    o_rs,
):
    f32, bf16 = jnp.float32, jnp.bfloat16
    n_tis = 4 * n_z
    chunk = pts // n_ves
    quarter = segs // 4
    n_chunks = segs // LANES
    per_q = n_z
    total_pts = pts * n_tis
    total_segs = segs * n_ves
    t, v = lax.axis_index("tis"), lax.axis_index("ves")
    y, z, core = t // (2 * n_z), (t // 2) % n_z, t % 2

    def quarter_of(m):
        return ((y + m // 2) % 2) * 2 + (core + m % 2) % 2

    def tis_near(m):
        return ((y + m // 2) % 2) * (2 * n_z) + z * 2 + (core + m % 2) % 2

    def tis_along(k):
        return y * (2 * n_z) + ((z + k) % n_z) * 2 + core

    def ves_at(k):
        return (v + k) % n_ves

    def send_ves(k, a, b, s, r):
        return pltpu.make_async_remote_copy(
            src_ref=a, dst_ref=b, send_sem=s, recv_sem=r, device_id={"ves": ves_at(k)}, device_id_type=MESH
        )

    def send_tis(to, a, b, s, r):
        return pltpu.make_async_remote_copy(
            src_ref=a, dst_ref=b, send_sem=s, recv_sem=r, device_id={"tis": to}, device_id_type=MESH
        )

    def t_copy(it, k):
        return send_ves(k, t_send.at[k], t_recv.at[it, k - 1], t_ss.at[k - 1], t_rs.at[it, k - 1])

    def l_copy(it, k, of):
        return send_ves(k, level.at[it, of], level.at[it, of], l_ss.at[k - 1], l_rs.at[it, k - 1])

    def a_copy(it, m):
        return send_tis(tis_near(m), a_send.at[m], a_recv.at[it, m - 1], a_ss.at[m - 1], a_rs.at[it, m - 1])

    def b_copy(it, k):
        return send_tis(
            tis_along(k), b_send.at[(z + k) % n_z], b_recv.at[it, k - 1], b_ss.at[k - 1], b_rs.at[it, k - 1]
        )

    def z_copy(it, k, of):
        place = src.at[it + 1, quarter_of(0), of]
        return send_tis(tis_along(k), place, place, z_ss.at[k - 1], z_rs.at[it, k - 1])

    def c_copy(it, m, of):
        place = src.at[it + 1, of]
        return send_tis(tis_near(m), place, place, c_ss.at[m - 1], c_rs.at[it, m - 1])

    def o_copy(it):
        return send_ves(
            1, joined.at[it, pl.ds(n_chunks, n_chunks)], joined.at[it, pl.ds(0, n_chunks)], o_ss.at[0], o_rs.at[it]
        )

    barrier = pltpu.get_barrier_semaphore()

    def greet_ves(k, carry):
        pl.semaphore_signal(barrier, 1, device_id={"ves": ves_at(k)}, device_id_type=MESH)
        return carry

    def greet_near(m, carry):
        pl.semaphore_signal(barrier, 1, device_id={"tis": tis_near(m)}, device_id_type=MESH)
        return carry

    def greet_along(k, carry):
        pl.semaphore_signal(barrier, 1, device_id={"tis": tis_along(k)}, device_id_type=MESH)
        return carry

    lax.fori_loop(1, n_ves, greet_ves, 0)
    lax.fori_loop(1, 4, greet_near, 0)
    lax.fori_loop(1, n_z, greet_along, 0)

    solute = lax.broadcasted_iota(jnp.int32, (8, LANES), 0)
    lane = lax.broadcasted_iota(jnp.int32, (8, LANES), 1)

    def column(ref):
        out = jnp.zeros((8, LANES), f32)
        for s in range(8):
            out = jnp.where(solute == s, ref[s], out)
        return out

    half = column(half_ref)[:, :1]
    diff = column(diff_ref)[:, :1]
    base[...] = column(base_ref)

    feat[...] = jnp.zeros_like(feat)
    square = jnp.zeros((1, pts), f32)
    for d in range(3):
        p = point_ref[d : d + 1, :] - 0.5
        square = square + p * p
        for a, piece in enumerate(pieces(p)):
            for b in range(3):
                row = 9 * d + 3 * a + b
                feat[row : row + 1, :pts] = piece
    for a, piece in enumerate(pieces(square)):
        feat[27 + a : 28 + a, :pts] = piece
        feat[30 + a : 31 + a, :pts] = jnp.ones((1, pts), f32)

    def turn(i, carry):
        point_feat[at(i, LANES), :] = feat[:, at(i, LANES)].T.astype(bf16)
        return carry

    lax.fori_loop(0, pts // LANES, turn, 0)

    square = radius_ref[...] * radius_ref[...]
    for d in range(3):
        s = seg_ref[d : d + 1, :] - 0.5
        square = square + s * s
        for b, piece in enumerate(pieces(s)):
            for a in range(3):
                row = 9 * d + 3 * a + b
                feat[row : row + 1, :segs] = -2.0 * piece
    for a, piece in enumerate(pieces(square)):
        feat[27 + a : 28 + a, :segs] = jnp.ones((1, segs), f32)
        feat[30 + a : 31 + a, :segs] = piece
    seg_feat[...] = feat[:, :segs].astype(bf16)

    table = table_ref[...]
    for i in range(pts // LANES):
        cell = jnp.broadcast_to(cell_ref[:, i * LANES : (i + 1) * LANES], (8, LANES))
        rates[:, i * LANES : (i + 1) * LANES] = jnp.take_along_axis(table, cell, axis=1)

    total = jnp.zeros((8, LANES), f32)
    for i in range(n_chunks):
        cols = slice(i * LANES, (i + 1) * LANES)
        own, held = sources_ref[:, cols], contents_ref[:, cols]
        src[0, i // per_q, i % per_q] = own
        cont[i] = held
        joined[0, n_chunks + i] = held - own * flow_ref[:, cols]
        total = total + own
    for k in range(n_ves):
        t_send[k, :, chunk:] = total

    def build(k, carry):
        of = ves_at(k % n_ves)
        rows = at(of, chunk)
        block = lax.rsqrt(dot(point_feat[rows, :], seg_feat[...])).astype(bf16)
        tile[rows, :] = block
        t_send[k % n_ves, :, :chunk] = dot_nt(sources_ref[...].astype(bf16), block)

        @pl.when(k == 1)
        def _():
            pl.semaphore_wait(barrier, n_ves - 1 + 3 + n_z - 1)
            o_copy(0).start()

        @pl.when(k < n_ves)
        def _():
            t_copy(0, k).start()

        return carry

    lax.fori_loop(1, n_ves + 1, build, 0)

    def sweep(it, carry):
        o_copy(it).wait()

        def gather(c, carry):
            cols = at(c, LANES)
            parent = jnp.broadcast_to(parent_ref[:, cols], (8, LANES))
            root = parent == v * segs + c * LANES + lane
            offset = parent - (v * segs - segs) - c * LANES
            which, place = offset >> 7, offset & (LANES - 1)
            found = jnp.zeros((8, LANES), f32)
            for h in range(n_chunks + 1):
                found = jnp.where(which == h, jnp.take_along_axis(joined[it, c + h], place, axis=1), found)
            cont[c] = jnp.where(root, inflow_ref[:, cols], found)
            return carry

        lax.fori_loop(0, n_chunks, gather, 0)

        summed = t_send[0]
        for k in range(1, n_ves):
            t_copy(it, k).wait()
            summed = summed + t_recv[it, k - 1]
        level[it, v] = base[:, :1] + summed[:, :chunk] / (diff * total_segs)

        def share(k, carry):
            l_copy(it, k, v).start()
            return carry

        lax.fori_loop(1, n_ves, share, 0)
        sink_sum[...] = jnp.zeros_like(sink_sum)

        def sink_of(k):
            of = (v + n_ves - k) % n_ves

            @pl.when(k > 0)
            def _():
                l_copy(it, k, of).wait()

            now = level[it, of]
            value = rates[:, at(of, chunk)] * now / (jnp.abs(now) + half)
            sink[k] = value
            part = value[:, :LANES]
            for i in range(1, chunk // LANES):
                part = part + value[:, i * LANES : (i + 1) * LANES]
            sink_sum[...] += part
            return of

        wall[...] = jnp.zeros_like(wall)

        def early(k, carry):
            of = sink_of(k)
            wall[...] += dot(sink[k].astype(bf16), tile[at(of, chunk), :])
            return carry

        def late(k, carry):
            sink_of(k)
            return carry

        lax.fori_loop(0, n_ves // 2, early, 0)
        lax.fori_loop(n_ves // 2, n_ves, late, 0)

        def finish(i, carry):
            m = 3 - i
            cols = at(quarter_of(m), quarter)
            part = wall[:, cols]
            for k in range(n_ves // 2, n_ves):
                of = (v + n_ves - k) % n_ves
                part = part + dot(sink[k].astype(bf16), tile[at(of, chunk), cols])
            a_send[m, :, :quarter] = part
            a_send[m, :, quarter:] = sink_sum[...]

            @pl.when(m > 0)
            def _():
                a_copy(it, m).start()

            return carry

        lax.fori_loop(0, 4, finish, 0)
        own = a_send[0]
        for m in range(1, 4):
            a_copy(it, m).wait()
            own = own + a_recv[it, m - 1]
        for i in range(n_z):
            b_send[i, :, :LANES] = own[:, i * LANES : (i + 1) * LANES]
            b_send[i, :, LANES:] = own[:, quarter:]

        def spread(k, carry):
            b_copy(it, k).start()
            return carry

        lax.fori_loop(1, n_z, spread, 0)
        own = b_send[z]
        for k in range(1, n_z):
            b_copy(it, k).wait()
            own = own + b_recv[it, k - 1]
        q = quarter_of(0)
        cols = at(q * per_q + z, LANES)
        wall_field = own[:, :LANES] / (diff * total_pts)
        src[it + 1, q, z] = RELAX * src[it, q, z] + RELAX * cond_ref[:, cols] * (cont[q * per_q + z] - wall_field)

        def along(k, carry):
            z_copy(it, k, z).start()
            return carry

        lax.fori_loop(1, n_z, along, 0)
        source_total = jnp.sum(summed[:, chunk:], axis=1, keepdims=True)
        sink_total = jnp.sum(own[:, LANES:], axis=1, keepdims=True)
        base[...] += BALANCE * (source_total / total_segs - sink_total / total_pts)
        for k in range(1, n_z):
            z_copy(it, k, (z + n_z - k) % n_z).wait()

        def beside(m, carry):
            c_copy(it, m, q).start()
            return carry

        lax.fori_loop(1, 4, beside, 0)

        def source_block(of):
            return jnp.concatenate([src[it + 1, of, i] for i in range(per_q)], axis=1).astype(bf16)

        @pl.when(it < ITERS - 1)
        def _():
            rows_at_once = pts // 4

            def first(i, carry):
                rows = at(i, rows_at_once)
                t_sum[:, rows] = dot_nt(source_block(q), tile[rows, at(q, quarter)])
                return carry

            lax.fori_loop(0, 4, first, 0)

            def middle(m, carry):
                of = quarter_of(m)
                c_copy(it, m, of).wait()

                def some(i, carry):
                    rows = at(i, rows_at_once)
                    t_sum[:, rows] += dot_nt(source_block(of), tile[rows, at(of, quarter)])
                    return carry

                return lax.fori_loop(0, 4, some, carry)

            lax.fori_loop(1, 3, middle, 0)
            of = quarter_of(3)
            c_copy(it, 3, of).wait()

            total = jnp.zeros((8, LANES), f32)
            for i in range(n_chunks):
                cols = slice(i * LANES, (i + 1) * LANES)
                now = src[it + 1, i // per_q, i % per_q]
                joined[it + 1, n_chunks + i] = cont[i] - now * flow_ref[:, cols]
                total = total + now
            for k in range(n_ves):
                t_send[k, :, chunk:] = total
            o_copy(it + 1).start()

            def last(k, carry):
                rows = at(ves_at(k % n_ves), chunk)
                t_send[k % n_ves, :, :chunk] = t_sum[:, rows] + dot_nt(
                    source_block(of), tile[rows, at(of, quarter)]
                )

                @pl.when(k < n_ves)
                def _():
                    t_copy(it + 1, k).start()

                return carry

            lax.fori_loop(1, n_ves + 1, last, 0)

        @pl.when(it == ITERS - 1)
        def _():
            for i in range(n_ves):
                level_out[:, i * chunk : (i + 1) * chunk] = level[it, i]
            for i in range(n_chunks):
                contents_out[:, i * LANES : (i + 1) * LANES] = cont[i]
            for m in range(1, 4):
                c_copy(it, m, quarter_of(m)).wait()
            for i in range(n_chunks):
                sources_out[:, i * LANES : (i + 1) * LANES] = src[it + 1, i // per_q, i % per_q]

        return carry

    lax.fori_loop(0, ITERS, sweep, 0)


def body(
    point_xyz,
    point_cell,
    seg_xyz,
    seg_radius,
    conductance,
    flow_inv,
    parent,
    inflow,
    rate_table,
    half_sat,
    diffusivity,
    base_level,
    sources,
    contents,
):
    n_ves = lax.axis_size("ves")
    n_z = lax.axis_size("tis") // 4
    pts, segs = point_xyz.shape[1], seg_xyz.shape[1]
    chunk, quarter, n_chunks = pts // n_ves, segs // 4, segs // LANES
    f32, bf16 = jnp.float32, jnp.bfloat16
    vmem = pl.BlockSpec(memory_space=pltpu.VMEM)
    smem = pl.BlockSpec(memory_space=pltpu.SMEM)
    sem = pltpu.SemaphoreType.DMA
    line = lambda x: x.reshape(1, -1)
    return pl.pallas_call(
        functools.partial(kernel, n_ves, n_z, pts, segs),
        out_shape=(
            jax.ShapeDtypeStruct((8, pts), f32),
            jax.ShapeDtypeStruct((8, segs), f32),
            jax.ShapeDtypeStruct((8, segs), f32),
        ),
        in_specs=[vmem] * 9 + [smem] * 3 + [vmem] * 2,
        out_specs=(vmem, vmem, vmem),
        scratch_shapes=[
            pltpu.VMEM((pts, segs), bf16),
            pltpu.VMEM((pts, FEATURES), bf16),
            pltpu.VMEM((FEATURES, segs), bf16),
            pltpu.VMEM((FEATURES, max(pts, segs)), f32),
            pltpu.VMEM((8, pts), f32),
            pltpu.VMEM((8, LANES), f32),
            pltpu.VMEM((8, pts), f32),
            pltpu.VMEM((n_ves, 8, chunk + LANES), f32),
            pltpu.VMEM((ITERS, n_ves - 1, 8, chunk + LANES), f32),
            pltpu.VMEM((ITERS, n_ves, 8, chunk), f32),
            pltpu.VMEM((n_ves, 8, chunk), f32),
            pltpu.VMEM((8, LANES), f32),
            pltpu.VMEM((8, segs), f32),
            pltpu.VMEM((4, 8, quarter + LANES), f32),
            pltpu.VMEM((ITERS, 3, 8, quarter + LANES), f32),
            pltpu.VMEM((n_z, 8, 2 * LANES), f32),
            pltpu.VMEM((ITERS, n_z - 1, 8, 2 * LANES), f32),
            pltpu.VMEM((ITERS + 1, 4, n_z, 8, LANES), f32),
            pltpu.VMEM((n_chunks, 8, LANES), f32),
            pltpu.VMEM((ITERS, 2 * n_chunks, 8, LANES), f32),
            sem((n_ves - 1,)),
            sem((ITERS, n_ves - 1)),
            sem((n_ves - 1,)),
            sem((ITERS, n_ves - 1)),
            sem((3,)),
            sem((ITERS, 3)),
            sem((n_z - 1,)),
            sem((ITERS, n_z - 1)),
            sem((n_z - 1,)),
            sem((ITERS, n_z - 1)),
            sem((3,)),
            sem((ITERS, 3)),
            sem((1,)),
            sem((ITERS,)),
        ],
        compiler_params=pltpu.CompilerParams(
            collective_id=0, has_side_effects=True, vmem_limit_bytes=60 * 2**20
        ),
        name="exchange",
    )(
        point_xyz,
        line(point_cell),
        seg_xyz,
        line(seg_radius),
        line(conductance),
        line(flow_inv),
        line(parent),
        inflow,
        rate_table,
        half_sat,
        diffusivity,
        base_level,
        sources,
        contents,
    )


def solution(mesh):
    return jax.shard_map(
        body,
        mesh=mesh,
        in_specs=(
            P(None, "tis"),
            P("tis"),
            P(None, "ves"),
            P("ves"),
            P("ves"),
            P("ves"),
            P("ves"),
            P(None, "ves"),
            P(),
            P(),
            P(),
            P(),
            P(None, "ves"),
            P(None, "ves"),
        ),
        out_specs=(P(None, "tis"), P(None, "ves"), P(None, "ves")),
        check_vma=False,
    )
```

time: 343 us -> 136 us (0.40)
  Pallas kernels: 0 us -> 132 us
  matrix products: 83.4 us -> 0 us
  waiting for transfers between devices: 72.2 us -> 0 us
  local copies, waits for them, and re-layouts: 73.6 us -> 3.21 us
  starting transfers between devices: 65.2 us -> 0 us
  other arithmetic: 45.3 us -> 0 us
    pallas_call x0 -> x1, Pallas kernels: none -> 132 us  [body(): pl.pallas_call(functools.partial(kernel, n_ves, n_z, pts, segs), out_shap...]
    dot_general x7 -> x0, matrix products: 83.4 us -> none  [the longest x3 44.1 us: body(): lax.dot_general(src_bf, kernel_tiles, dims_rows, preferred_element_type=j...]
    all_to_all x9 -> x0, waiting for transfers between devices: 72.2 us -> none  [the longest x6 48.7 us: copy_for_each(): return lax.all_to_all(copies, axis, split_axis=0, concat_axis=0, tiled=True)]
    all_to_all x9 -> x0, starting transfers between devices: 56.9 us -> none  [the longest x6 30 us: copy_for_each(): return lax.all_to_all(copies, axis, split_axis=0, concat_axis=0, tiled=True)]
    gather x6 -> x0, local copies, waits for them, and re-layouts: 40.5 us -> none  [body(): fetched = jnp.take(joined, local_parent, axis=1)]
    dynamic_update_slice x8 -> x0, other arithmetic: 38.1 us -> none  [body(): lax.map(lambda pts_block: kernel_rows(pts_block, seg_xyz, seg_radius), po...]
    slice x22 -> x0, local copies, waits for them, and re-layouts: 14.6 us -> none  [the longest x16 14.5 us: kernel_rows(): dist_sq = (points[0][:, None] - seg_pos[0][None, :]) ** 2]
    ppermute x3 -> x0, starting transfers between devices: 8.33 us -> none  [from_behind(): lax.ppermute(value, axis, [(source, source + steps) for source in range(l...]
  transfers between devices with their start and end apart: 12 -> 0, of which waited for: 6 -> 0; matrix products, arithmetic and copies ran while one was open for 19% -> 0% of each run, Pallas kernels for 0% -> 0%
where the time goes in v1:
time: 136 us
  Pallas kernels  132 us (97%)
  local copies, waits for them, and re-layouts  3.21 us (2%)
    pallas_call x1, Pallas kernels, body(): pl.pallas_call(functools.partial(kernel, n_ves, n_z, pts, segs), out_shap...  132 us
    unnamed x7, local copies, waits for them, and re-layouts  3.21 us

profile of v1, /device:TPU:1, one launch (start us, length us, event | category | flops | bytes accessed | tf_op | source)
XLA Modules:
  0.0 135.9 jit_solution(11664999959340395704)
XLA Ops:
  0.6 132.0 %exchange.1 = (f32[8,4096]{1,0:T(8,128)}, f32[8,4096]{1,0:T(8,128)}, f32[8,4096]{1,0:T(8,128)}) custom-call(f32[3,4096]{1,0:T(4,128)} %point_ref.1, s32[1,4096]{1,0:T(1,128)} %bitcast.5, f32[3,4096]{1,0:T(4,128)} %seg_ref.1, f32[1,4096]{1,0:T(1,128)} %bitcast.6, f32[1,4096]{1,0:T(1,128)} %bitcast.7, f32[1,4096]{1,0:T(1,128)} %bitcast.8, s32[1,4096]{1,0:T(1,128)} %bitcast.9, ...), custom_call_target="tpu_custom_call" | custom-call | tf_op jit(solution)/shard_map/exchange/pallas_call | solution.py:463
  132.6 0.0 copy-start.1
  132.6 1.6 %copy.20 = f32[8,4096]{1,0:T(8,128)} copy(f32[8,4096]{1,0:T(8,128)} %get-tuple-element.6) | data formatting | bytes 262144
  134.2 0.0 copy-done.1
  134.2 0.0 copy-start
  134.2 0.7 copy.21
  134.9 0.3 copy-done
  135.2 0.7 copy.22
Async XLA Ops:
  132.6 1.6 %copy-start.1 = (f32[8,4096]{1,0:T(8,128)S(1)}, f32[8,4096]{1,0:T(8,128)}, u32[]{:S(2)}) copy-start(f32[8,4096]{1,0:T(8,128)} %get-tuple-element.7) | copy-start | bytes 393220
  134.2 1.0 copy-start

commit v2 on v1

v2 whole, which is shorter than its diff:
```python
import functools

import jax
import jax.numpy as jnp
from jax import lax
from jax.experimental import pallas as pl
from jax.experimental.pallas import tpu as pltpu
from jax.sharding import PartitionSpec as P

ITERS = 3
RELAX = 0.5
BALANCE = 0.5
LANES = 128
FEATURES = 48
MESH = pl.DeviceIdType.MESH


def pieces(x):
    high = x.astype(jnp.bfloat16).astype(jnp.float32)
    rest = x - high
    middle = rest.astype(jnp.bfloat16).astype(jnp.float32)
    return high, middle, (rest - middle).astype(jnp.bfloat16).astype(jnp.float32)


def dot(a, b):
    return jnp.dot(a, b, preferred_element_type=jnp.float32)


def dot_nt(a, b):
    return lax.dot_general(a, b, (((1,), (1,)), ((), ())), preferred_element_type=jnp.float32)


def at(i, size):
    return pl.ds(pl.multiple_of(i * size, size), size)


def kernel(
    n_ves,
    n_z,
    pts,
    segs,
    point_ref,
    cell_ref,
    seg_ref,
    radius_ref,
    cond_ref,
    flow_ref,
    parent_ref,
    inflow_ref,
    table_ref,
    half_ref,
    diff_ref,
    base_ref,
    sources_ref,
    contents_ref,
    level_out,
    sources_out,
    contents_out,
    tile,
    point_feat,
    seg_feat,
    feat,
    feat_seg,
    rates,
    base,
    t_sum,
    t_send,
    t_recv,
    level,
    sink,
    sink_sum,
    wall,
    a_send,
    a_recv,
    b_send,
    b_recv,
    src,
    cont,
    joined,
    t_ss,
    t_rs,
    l_ss,
    l_rs,
    a_ss,
    a_rs,
    b_ss,
    b_rs,
    z_ss,
    z_rs,
    c_ss,
    c_rs,
    o_ss,
    o_rs,
):
    f32, bf16 = jnp.float32, jnp.bfloat16
    n_tis = 4 * n_z
    chunk = pts // n_ves
    quarter = segs // 4
    n_chunks = segs // LANES
    per_q = n_z
    total_pts = pts * n_tis
    total_segs = segs * n_ves
    t, v = lax.axis_index("tis"), lax.axis_index("ves")
    y, z, core = t // (2 * n_z), (t // 2) % n_z, t % 2

    def quarter_of(core, y):
        return core % 2 * 2 + y % 2

    def tis_at(k):
        return ((y + k // n_z) % 2) * (2 * n_z) + ((z + k % n_z) % n_z) * 2 + core

    other_core = y * (2 * n_z) + z * 2 + (core + 1) % 2

    n_x = n_ves // 2
    n_pairs = n_z // 2
    v_y, v_x = v // n_x, v % n_x

    def ves_at(k):
        return ((v_y + k // n_x) % 2) * n_x + (v_x + k % n_x) % n_x

    def ves_from(k):
        return ((v_y + k // n_x) % 2) * n_x + (v_x + n_x - k % n_x) % n_x

    far_first = sorted(range(1, 2 * n_z), key=lambda k: -(k // n_z) - min(k % n_z, n_z - k % n_z))
    near_first = sorted(range(n_pairs), key=lambda k: min(k, n_pairs - k))

    def send_ves(k, a, b, s, r):
        return pltpu.make_async_remote_copy(
            src_ref=a, dst_ref=b, send_sem=s, recv_sem=r, device_id={"ves": ves_at(k)}, device_id_type=MESH
        )

    def send_tis(to, a, b, s, r):
        return pltpu.make_async_remote_copy(
            src_ref=a, dst_ref=b, send_sem=s, recv_sem=r, device_id={"tis": to}, device_id_type=MESH
        )

    def t_copy(it, k):
        return send_ves(k, t_send.at[k], t_recv.at[it, k - 1], t_ss.at[k - 1], t_rs.at[it, k - 1])

    def l_copy(it, k, of):
        return send_ves(k, level.at[it, of], level.at[it, of], l_ss.at[k - 1], l_rs.at[it, k - 1])

    def a_copy(it, i):
        return send_tis(other_core, a_send.at[i], a_recv.at[it, i], a_ss.at[i], a_rs.at[it, i])

    def b_copy(it, k):
        block = b_send.at[(y + k // n_z) % 2, (z + k % n_z) % n_z]
        return send_tis(tis_at(k), block, b_recv.at[it, k - 1], b_ss.at[k - 1], b_rs.at[it, k - 1])

    def z_copy(it, k, q, of):
        place = src.at[it + 1, q, of]
        return send_tis(tis_at(k), place, place, z_ss.at[k - 1], z_rs.at[it, k - 1])

    def c_copy(it, i, q):
        place = src.at[it + 1, q]
        return send_tis(other_core, place, place, c_ss.at[i], c_rs.at[it, i])

    def o_copy(it):
        return pltpu.make_async_remote_copy(
            src_ref=joined.at[it, pl.ds(n_chunks, n_chunks)],
            dst_ref=joined.at[it, pl.ds(0, n_chunks)],
            send_sem=o_ss.at[0],
            recv_sem=o_rs.at[it],
            device_id={"ves": (v + 1) % n_ves},
            device_id_type=MESH,
        )

    barrier = pltpu.get_barrier_semaphore()

    def greet_ves(k, carry):
        pl.semaphore_signal(barrier, 1, device_id={"ves": ves_at(k)}, device_id_type=MESH)
        return carry

    def greet_tis(k, carry):
        pl.semaphore_signal(barrier, 1, device_id={"tis": tis_at(k)}, device_id_type=MESH)
        return carry

    lax.fori_loop(1, n_ves, greet_ves, 0)
    lax.fori_loop(1, 2 * n_z, greet_tis, 0)
    pl.semaphore_signal(barrier, 1, device_id={"tis": other_core}, device_id_type=MESH)

    solute = lax.broadcasted_iota(jnp.int32, (8, LANES), 0)
    lane = lax.broadcasted_iota(jnp.int32, (8, LANES), 1)

    def column(ref):
        out = jnp.zeros((8, LANES), f32)
        for s in range(8):
            out = jnp.where(solute == s, ref[s], out)
        return out

    half = column(half_ref)[:, :1]
    diff = column(diff_ref)[:, :1]
    base[...] = column(base_ref)

    feat[...] = jnp.zeros_like(feat)
    feat_seg[...] = jnp.zeros_like(feat_seg)
    square = jnp.zeros((1, pts), f32)
    for d in range(3):
        p = point_ref[d : d + 1, :] - 0.5
        square = square + p * p
        for a, piece in enumerate(pieces(p)):
            for b in range(3):
                row = 9 * d + 3 * a + b
                feat[row : row + 1, :] = piece
    for a, piece in enumerate(pieces(square)):
        feat[27 + a : 28 + a, :] = piece
        feat[30 + a : 31 + a, :] = jnp.ones((1, pts), f32)

    def turn(k):
        for i in range(chunk // LANES):
            cols = at(ves_at(k) * (chunk // LANES) + i, LANES)
            point_feat[cols, :] = feat[:, cols].T.astype(bf16)

    turn(n_ves - 1)

    square = radius_ref[...] * radius_ref[...]
    for d in range(3):
        s = seg_ref[d : d + 1, :] - 0.5
        square = square + s * s
        for b, piece in enumerate(pieces(s)):
            for a in range(3):
                row = 9 * d + 3 * a + b
                feat_seg[row : row + 1, :] = -2.0 * piece
    for a, piece in enumerate(pieces(square)):
        feat_seg[27 + a : 28 + a, :] = jnp.ones((1, segs), f32)
        feat_seg[30 + a : 31 + a, :] = piece
    seg_feat[...] = feat_seg[...].astype(bf16)

    table = table_ref[...]
    for i in range(pts // LANES):
        cell = jnp.broadcast_to(cell_ref[:, i * LANES : (i + 1) * LANES], (8, LANES))
        rates[:, i * LANES : (i + 1) * LANES] = jnp.take_along_axis(table, cell, axis=1)

    total = jnp.zeros((8, LANES), f32)
    for i in range(n_chunks):
        cols = slice(i * LANES, (i + 1) * LANES)
        own, held = sources_ref[:, cols], contents_ref[:, cols]
        src[0, i // per_q, i % per_q] = own
        cont[i] = held
        joined[0, n_chunks + i] = held - own * flow_ref[:, cols]
        total = total + own
    for k in range(n_ves):
        t_send[k, :, chunk:] = total

    def build(i, carry):
        k = n_ves - 1 - i
        rows = at(ves_at(k), chunk)
        turn((k + n_ves - 1) % n_ves)
        block = lax.rsqrt(dot(point_feat[rows, :], seg_feat[...])).astype(bf16)
        tile[rows, :] = block
        t_send[k, :, :chunk] = dot_nt(sources_ref[...].astype(bf16), block)

        @pl.when(i == 0)
        def _():
            pl.semaphore_wait(barrier, n_ves - 1 + 2 * n_z)

        @pl.when(k > 0)
        def _():
            t_copy(0, k).start()

        return carry

    lax.fori_loop(0, n_ves, build, 0)

    def sweep(it, carry):
        summed = t_send[0]
        for k in range(1, n_ves):
            t_copy(it, k).wait()
            summed = summed + t_recv[it, k - 1]
        level[it, v] = base[:, :1] + summed[:, :chunk] / (diff * total_segs)

        def share(i, carry):
            l_copy(it, n_ves - 1 - i, v).start()
            return carry

        lax.fori_loop(0, n_ves - 1, share, 0)
        o_copy(it).start()
        sink_sum[...] = jnp.zeros_like(sink_sum)

        def sink_of(k):
            of = ves_from(k)

            @pl.when(k > 0)
            def _():
                l_copy(it, k, of).wait()

            now = level[it, of]
            value = rates[:, at(of, chunk)] * now / (jnp.abs(now) + half)
            sink[k] = value
            part = value[:, :LANES]
            for i in range(1, chunk // LANES):
                part = part + value[:, i * LANES : (i + 1) * LANES]
            sink_sum[...] += part
            return of

        wall[...] = jnp.zeros_like(wall)

        def early(k, carry):
            of = sink_of(k)
            wall[...] += dot(sink[k].astype(bf16), tile[at(of, chunk), :])
            return carry

        def late(k, carry):
            sink_of(k)
            return carry

        lax.fori_loop(0, n_ves // 2, early, 0)
        lax.fori_loop(n_ves // 2, n_ves, late, 0)

        sums = jnp.sum(sink_sum[...], axis=1, keepdims=True)
        sink_row = jnp.sum(jnp.where(solute == lane, sums, 0.0), axis=0, keepdims=True)
        for i in range(4):
            a_send[i, :, quarter:] = jnp.broadcast_to(sink_row, (8, LANES))

        def finish(i, carry):
            cols = at(quarter_of(core + 1 + i // 2, i), quarter)
            part = wall[:, cols]
            for k in range(n_ves // 2, n_ves):
                of = ves_from(k)
                part = part + dot(sink[k].astype(bf16), tile[at(of, chunk), cols])
            a_send[i, :, :quarter] = part

            @pl.when(i < 2)
            def _():
                a_copy(it, i).start()

            return carry

        lax.fori_loop(0, 4, finish, 0)
        for h in range(2):
            a_copy(it, h).wait()
            own = a_send[2 + h] + a_recv[it, h]
            for i in range(n_z):
                b_send[h, i, :8, :] = own[:, i * LANES : (i + 1) * LANES]
                b_send[h, i, 8:, :] = own[:1, quarter:]

        for k in far_first:
            b_copy(it, k).start()

        o_copy(it).wait()

        def gather(c, carry):
            cols = at(c, LANES)
            parent = jnp.broadcast_to(parent_ref[:, cols], (8, LANES))
            root = parent == v * segs + c * LANES + lane
            offset = parent - (v * segs - segs) - c * LANES
            which, place = offset >> 7, offset & (LANES - 1)
            found = jnp.zeros((8, LANES), f32)
            for h in range(n_chunks + 1):
                found = jnp.where(which == h, jnp.take_along_axis(joined[it, c + h], place, axis=1), found)
            cont[c] = jnp.where(root, inflow_ref[:, cols], found)
            return carry

        lax.fori_loop(0, n_chunks, gather, 0)

        own = b_send[y, z]
        for k in range(1, 2 * n_z):
            b_copy(it, k).wait()
            own = own + b_recv[it, k - 1]
        q = quarter_of(core, y)
        cols = at(q * per_q + z, LANES)
        wall_field = own[:8] / (diff * total_pts)
        src[it + 1, q, z] = RELAX * src[it, q, z] + RELAX * cond_ref[:, cols] * (cont[q * per_q + z] - wall_field)
        for k in far_first:
            z_copy(it, k, q, z).start()
        source_total = jnp.sum(summed[:, chunk:], axis=1, keepdims=True)
        sink_total = jnp.sum(jnp.where(solute == lane, own[8:], 0.0), axis=1, keepdims=True)
        base[...] += BALANCE * (source_total / total_segs - sink_total / total_pts)

        def source_block(of):
            return jnp.concatenate([src[it + 1, of, i] for i in range(per_q)], axis=1).astype(bf16)

        for step in range(2 * n_pairs):
            from_y = (y + step // n_pairs) % 2
            pair = (z // 2 + near_first[step % n_pairs]) % n_pairs
            q = quarter_of(core, from_y)
            for e in range(2):
                of = pair * 2 + e
                k = (step // n_pairs) * n_z + (z + n_z - of) % n_z

                @pl.when(k > 0)
                def _():
                    z_copy(it, k, q, of).wait()

            if step % n_pairs == n_pairs - 1:
                c_copy(it, step // n_pairs, q).start()

            @pl.when(it < ITERS - 1)
            def _():
                two = jnp.concatenate([src[it + 1, q, pair * 2], src[it + 1, q, pair * 2 + 1]], axis=1).astype(bf16)
                part = dot_nt(two, tile[:, pl.ds(pl.multiple_of(q * quarter + pair * 2 * LANES, LANES), 2 * LANES)])
                if step == 0:
                    t_sum[...] = part
                else:
                    t_sum[...] += part

        @pl.when(it < ITERS - 1)
        def _():
            of = quarter_of(core + 1, y)
            c_copy(it, 0, of).wait()
            t_sum[...] += dot_nt(source_block(of), tile[:, at(of, quarter)])
            of = quarter_of(core + 1, y + 1)
            c_copy(it, 1, of).wait()

            total = jnp.zeros((8, LANES), f32)
            for i in range(n_chunks):
                cols = slice(i * LANES, (i + 1) * LANES)
                now = src[it + 1, i // per_q, i % per_q]
                joined[it + 1, n_chunks + i] = cont[i] - now * flow_ref[:, cols]
                total = total + now
            for k in range(n_ves):
                t_send[k, :, chunk:] = total

            def last(i, carry):
                k = n_ves - 1 - i
                rows = at(ves_at(k), chunk)
                t_send[k, :, :chunk] = t_sum[:, rows] + dot_nt(
                    source_block(of), tile[rows, at(of, quarter)]
                )

                @pl.when(k > 0)
                def _():
                    t_copy(it + 1, k).start()

                return carry

            lax.fori_loop(0, n_ves, last, 0)

        @pl.when(it == ITERS - 1)
        def _():
            for i in range(n_ves):
                level_out[:, i * chunk : (i + 1) * chunk] = level[it, i]
            for i in range(n_chunks):
                contents_out[:, i * LANES : (i + 1) * LANES] = cont[i]
            for i in range(2):
                c_copy(it, i, quarter_of(core + 1, y + i)).wait()
            for i in range(n_chunks):
                sources_out[:, i * LANES : (i + 1) * LANES] = src[it + 1, i // per_q, i % per_q]

        return carry

    lax.fori_loop(0, ITERS, sweep, 0)


def hand_over(a, b, c, a_out, b_out, c_out):
    a_out[...] = a[...]
    b_out[...] = b[...]
    c_out[...] = c[...]


def body(
    point_xyz,
    point_cell,
    seg_xyz,
    seg_radius,
    conductance,
    flow_inv,
    parent,
    inflow,
    rate_table,
    half_sat,
    diffusivity,
    base_level,
    sources,
    contents,
):
    n_ves = lax.axis_size("ves")
    n_z = lax.axis_size("tis") // 4
    pts, segs = point_xyz.shape[1], seg_xyz.shape[1]
    chunk, quarter, n_chunks = pts // n_ves, segs // 4, segs // LANES
    f32, bf16 = jnp.float32, jnp.bfloat16
    vmem = pl.BlockSpec(memory_space=pltpu.VMEM)
    smem = pl.BlockSpec(memory_space=pltpu.SMEM)
    sem = pltpu.SemaphoreType.DMA
    line = lambda x: x.reshape(1, -1)
    out = pl.pallas_call(
        functools.partial(kernel, n_ves, n_z, pts, segs),
        out_shape=(
            jax.ShapeDtypeStruct((8, pts), f32),
            jax.ShapeDtypeStruct((8, segs), f32),
            jax.ShapeDtypeStruct((8, segs), f32),
        ),
        in_specs=[vmem] * 9 + [smem] * 3 + [vmem] * 2,
        out_specs=(vmem, vmem, vmem),
        scratch_shapes=[
            pltpu.VMEM((pts, segs), bf16),
            pltpu.VMEM((pts, FEATURES), bf16),
            pltpu.VMEM((FEATURES, segs), bf16),
            pltpu.VMEM((FEATURES, pts), f32),
            pltpu.VMEM((FEATURES, segs), f32),
            pltpu.VMEM((8, pts), f32),
            pltpu.VMEM((8, LANES), f32),
            pltpu.VMEM((8, pts), f32),
            pltpu.VMEM((n_ves, 8, chunk + LANES), f32),
            pltpu.VMEM((ITERS, n_ves - 1, 8, chunk + LANES), f32),
            pltpu.VMEM((ITERS, n_ves, 8, chunk), f32),
            pltpu.VMEM((n_ves, 8, chunk), f32),
            pltpu.VMEM((8, LANES), f32),
            pltpu.VMEM((8, segs), f32),
            pltpu.VMEM((4, 8, quarter + LANES), f32),
            pltpu.VMEM((ITERS, 2, 8, quarter + LANES), f32),
            pltpu.VMEM((2, n_z, 9, LANES), f32),
            pltpu.VMEM((ITERS, 2 * n_z - 1, 9, LANES), f32),
            pltpu.VMEM((ITERS + 1, 4, n_z, 8, LANES), f32),
            pltpu.VMEM((n_chunks, 8, LANES), f32),
            pltpu.VMEM((ITERS, 2 * n_chunks, 8, LANES), f32),
            sem((n_ves - 1,)),
            sem((ITERS, n_ves - 1)),
            sem((n_ves - 1,)),
            sem((ITERS, n_ves - 1)),
            sem((2,)),
            sem((ITERS, 2)),
            sem((2 * n_z - 1,)),
            sem((ITERS, 2 * n_z - 1)),
            sem((2 * n_z - 1,)),
            sem((ITERS, 2 * n_z - 1)),
            sem((2,)),
            sem((ITERS, 2)),
            sem((1,)),
            sem((ITERS,)),
        ],
        compiler_params=pltpu.CompilerParams(
            collective_id=0, has_side_effects=True, vmem_limit_bytes=60 * 2**20
        ),
        name="exchange",
    )(
        point_xyz,
        line(point_cell),
        seg_xyz,
        line(seg_radius),
        line(conductance),
        line(flow_inv),
        line(parent),
        inflow,
        rate_table,
        half_sat,
        diffusivity,
        base_level,
        sources,
        contents,
    )
    return pl.pallas_call(
        hand_over,
        out_shape=tuple(jax.ShapeDtypeStruct(x.shape, f32) for x in out),
        in_specs=[vmem] * 3,
        out_specs=(vmem,) * 3,
        name="hand_over",
    )(*out)


def solution(mesh):
    return jax.shard_map(
        body,
        mesh=mesh,
        in_specs=(
            P(None, "tis"),
            P("tis"),
            P(None, "ves"),
            P("ves"),
            P("ves"),
            P("ves"),
            P("ves"),
            P(None, "ves"),
            P(),
            P(),
            P(),
            P(),
            P(None, "ves"),
            P(None, "ves"),
        ),
        out_specs=(P(None, "tis"), P(None, "ves"), P(None, "ves")),
        check_vma=False,
    )
```

time: 136 us -> 116 us (0.85)
  Pallas kernels: 132 us -> 115 us
  local copies, waits for them, and re-layouts: 3.21 us -> 0 us
    pallas_call x1, Pallas kernels: 132 us -> 113 us  [body(): pl.pallas_call(functools.partial(kernel, n_ves, n_z, pts, segs), out_shap...]
    unnamed x7 -> x0, local copies, waits for them, and re-layouts: 3.21 us -> none
    pallas_call x0 -> x1, Pallas kernels: none -> 1.78 us  [body(): pl.pallas_call(hand_over, out_shape=tuple((jax.ShapeDtypeStruct(x.shape,...]
where the time goes in v2:
time: 116 us
  Pallas kernels  115 us (99%)
    pallas_call x1, Pallas kernels, body(): pl.pallas_call(functools.partial(kernel, n_ves, n_z, pts, segs), out_shap...  113 us

profile of v2, /device:TPU:1, one launch (start us, length us, event | category | flops | bytes accessed | tf_op | source)
XLA Modules:
  0.0 115.7 jit_solution(3039354795751198197)
XLA Ops:
  0.6 113.2 %exchange.1 = (f32[8,4096]{1,0:T(8,128)}, f32[8,4096]{1,0:T(8,128)}, f32[8,4096]{1,0:T(8,128)}) custom-call(f32[3,4096]{1,0:T(4,128)} %point_ref.1, s32[1,4096]{1,0:T(1,128)} %bitcast.5, f32[3,4096]{1,0:T(4,128)} %seg_ref.1, f32[1,4096]{1,0:T(1,128)} %bitcast.6, f32[1,4096]{1,0:T(1,128)} %bitcast.7, f32[1,4096]{1,0:T(1,128)} %bitcast.8, s32[1,4096]{1,0:T(1,128)} %bitcast.9, ...), custom_call_target="tpu_custom_call" | custom-call | tf_op jit(solution)/shard_map/exchange/pallas_call | solution.py:476
  113.9 1.8 %hand_over.1 = (f32[8,4096]{1,0:T(8,128)}, f32[8,4096]{1,0:T(8,128)}, f32[8,4096]{1,0:T(8,128)}) custom-call(f32[8,4096]{1,0:T(8,128)} %get-tuple-element.6.a, f32[8,4096]{1,0:T(8,128)} %get-tuple-element.7.b, f32[8,4096]{1,0:T(8,128)} %get-tuple-element.8.c), custom_call_target="tpu_custom_call" | custom-call | tf_op jit(solution)/shard_map/hand_over/pallas_call | solution.py:542

commit v3 on v2

--- a/solution.py
+++ b/solution.py
@@ -11,7 +11,7 @@
 RELAX = 0.5
 BALANCE = 0.5
 LANES = 128
-FEATURES = 48
+FEATURES = 80
 MESH = pl.DeviceIdType.MESH
 
 
@@ -112,6 +112,7 @@
     other_core = y * (2 * n_z) + z * 2 + (core + 1) % 2
 
     n_x = n_ves // 2
+    n_early = n_ves - max(1, n_ves * 3 // 8)
     n_pairs = n_z // 2
     v_y, v_x = v // n_x, v % n_x
 
@@ -192,19 +193,18 @@
     diff = column(diff_ref)[:, :1]
     base[...] = column(base_ref)
 
-    feat[...] = jnp.zeros_like(feat)
-    feat_seg[...] = jnp.zeros_like(feat_seg)
-    square = jnp.zeros((1, pts), f32)
-    for d in range(3):
-        p = point_ref[d : d + 1, :] - 0.5
-        square = square + p * p
-        for a, piece in enumerate(pieces(p)):
+    def spread(out, rows, order):
+        rows = jnp.concatenate(rows + [jnp.zeros((3, rows[0].shape[1]), f32)], axis=0)
+        for a, piece in enumerate(pieces(rows)):
             for b in range(3):
-                row = 9 * d + 3 * a + b
-                feat[row : row + 1, :] = piece
-    for a, piece in enumerate(pieces(square)):
-        feat[27 + a : 28 + a, :] = piece
-        feat[30 + a : 31 + a, :] = jnp.ones((1, pts), f32)
+                block = 3 * a + b if order else 3 * b + a
+                out[8 * block : 8 * block + 8, :] = piece
+        out[72:, :] = jnp.zeros((8, rows.shape[1]), f32)
+
+    point = point_ref[...] - 0.5
+    spread(
+        feat, [point, jnp.sum(point * point, axis=0, keepdims=True), jnp.ones((1, pts), f32)], True
+    )
 
     def turn(k):
         for i in range(chunk // LANES):
@@ -213,54 +213,52 @@
 
     turn(n_ves - 1)
 
-    square = radius_ref[...] * radius_ref[...]
-    for d in range(3):
-        s = seg_ref[d : d + 1, :] - 0.5
-        square = square + s * s
-        for b, piece in enumerate(pieces(s)):
-            for a in range(3):
-                row = 9 * d + 3 * a + b
-                feat_seg[row : row + 1, :] = -2.0 * piece
-    for a, piece in enumerate(pieces(square)):
-        feat_seg[27 + a : 28 + a, :] = jnp.ones((1, segs), f32)
-        feat_seg[30 + a : 31 + a, :] = piece
+    segment = seg_ref[...] - 0.5
+    square = jnp.sum(segment * segment, axis=0, keepdims=True) + radius_ref[...] * radius_ref[...]
+    spread(feat_seg, [-2.0 * segment, jnp.ones((1, segs), f32), square], False)
     seg_feat[...] = feat_seg[...].astype(bf16)
 
+    total = jnp.zeros((8, LANES), f32)
+    for i in range(n_chunks):
+        cols = slice(i * LANES, (i + 1) * LANES)
+        total = total + sources_ref[:, cols]
+    for k in range(n_ves):
+        t_send[k, :, chunk:] = total
+
+    def build(i, carry):
+        k = n_ves - 1 - i
+        rows = at(ves_at(k), chunk)
+        turn((k + n_ves - 1) % n_ves)
+        part = jnp.zeros((8, chunk), f32)
+        for j in range(0, segs, quarter):
+            cols = slice(j, j + quarter)
+            block = lax.rsqrt(dot(point_feat[rows, :], seg_feat[:, cols])).astype(bf16)
+            tile[rows, cols] = block
+            part = part + dot_nt(sources_ref[:, cols].astype(bf16), block)
+        t_send[k, :, :chunk] = part
+
+        @pl.when(i == 0)
+        def _():
+            pl.semaphore_wait(barrier, n_ves - 1 + 2 * n_z)
+
+        @pl.when(k > 0)
+        def _():
+            t_copy(0, k).start()
+
+        return carry
+
+    lax.fori_loop(0, n_ves, build, 0)
     table = table_ref[...]
     for i in range(pts // LANES):
         cell = jnp.broadcast_to(cell_ref[:, i * LANES : (i + 1) * LANES], (8, LANES))
         rates[:, i * LANES : (i + 1) * LANES] = jnp.take_along_axis(table, cell, axis=1)
 
-    total = jnp.zeros((8, LANES), f32)
     for i in range(n_chunks):
         cols = slice(i * LANES, (i + 1) * LANES)
         own, held = sources_ref[:, cols], contents_ref[:, cols]
         src[0, i // per_q, i % per_q] = own
         cont[i] = held
         joined[0, n_chunks + i] = held - own * flow_ref[:, cols]
-        total = total + own
-    for k in range(n_ves):
-        t_send[k, :, chunk:] = total
-
-    def build(i, carry):
-        k = n_ves - 1 - i
-        rows = at(ves_at(k), chunk)
-        turn((k + n_ves - 1) % n_ves)
-        block = lax.rsqrt(dot(point_feat[rows, :], seg_feat[...])).astype(bf16)
-        tile[rows, :] = block
-        t_send[k, :, :chunk] = dot_nt(sources_ref[...].astype(bf16), block)
-
-        @pl.when(i == 0)
-        def _():
-            pl.semaphore_wait(barrier, n_ves - 1 + 2 * n_z)
-
-        @pl.when(k > 0)
-        def _():
-            t_copy(0, k).start()
-
-        return carry
-
-    lax.fori_loop(0, n_ves, build, 0)
 
     def sweep(it, carry):
         summed = t_send[0]
@@ -269,11 +267,8 @@
             summed = summed + t_recv[it, k - 1]
         level[it, v] = base[:, :1] + summed[:, :chunk] / (diff * total_segs)
 
-        def share(i, carry):
-            l_copy(it, n_ves - 1 - i, v).start()
-            return carry
-
-        lax.fori_loop(0, n_ves - 1, share, 0)
+        for k in range(n_ves - 1, 0, -1):
+            l_copy(it, k, v).start()
         o_copy(it).start()
         sink_sum[...] = jnp.zeros_like(sink_sum)
 
@@ -304,38 +299,53 @@
             sink_of(k)
             return carry
 
-        lax.fori_loop(0, n_ves // 2, early, 0)
-        lax.fori_loop(n_ves // 2, n_ves, late, 0)
+        for k in range(n_early):
+            early(k, 0)
+        for k in range(n_early, n_ves):
+            late(k, 0)
 
         sums = jnp.sum(sink_sum[...], axis=1, keepdims=True)
         sink_row = jnp.sum(jnp.where(solute == lane, sums, 0.0), axis=0, keepdims=True)
         for i in range(4):
             a_send[i, :, quarter:] = jnp.broadcast_to(sink_row, (8, LANES))
 
-        def finish(i, carry):
-            cols = at(quarter_of(core + 1 + i // 2, i), quarter)
+        def finish(i):
+            cols = at(quarter_of(core + 1 + i // 2, y + 1 + i), quarter)
             part = wall[:, cols]
-            for k in range(n_ves // 2, n_ves):
+            for k in range(n_early, n_ves):
                 of = ves_from(k)
                 part = part + dot(sink[k].astype(bf16), tile[at(of, chunk), cols])
             a_send[i, :, :quarter] = part
 
-            @pl.when(i < 2)
+        def give(i, carry):
+            finish(i)
+            a_copy(it, i).start()
+            return carry
+
+        for i in range(2):
+            give(i, 0)
+
+        def keep(i, carry):
+            finish(2 + i)
+            a_copy(it, i).wait()
+            own = a_send[2 + i] + a_recv[it, i]
+            for j in range(n_z):
+                b_send[(y + 1 + i) % 2, j, :8, :] = own[:, j * LANES : (j + 1) * LANES]
+                b_send[(y + 1 + i) % 2, j, 8:, :] = own[:1, quarter:]
+
+            @pl.when(i == 0)
             def _():
-                a_copy(it, i).start()
+                for k in far_first:
+                    if k >= n_z:
+                        b_copy(it, k).start()
 
             return carry
 
-        lax.fori_loop(0, 4, finish, 0)
-        for h in range(2):
-            a_copy(it, h).wait()
-            own = a_send[2 + h] + a_recv[it, h]
-            for i in range(n_z):
-                b_send[h, i, :8, :] = own[:, i * LANES : (i + 1) * LANES]
-                b_send[h, i, 8:, :] = own[:1, quarter:]
-
+        for i in range(2):
+            keep(i, 0)
         for k in far_first:
-            b_copy(it, k).start()
+            if k < n_z:
+                b_copy(it, k).start()
 
         o_copy(it).wait()
 
@@ -370,20 +380,19 @@
         def source_block(of):
             return jnp.concatenate([src[it + 1, of, i] for i in range(per_q)], axis=1).astype(bf16)
 
-        for step in range(2 * n_pairs):
-            from_y = (y + step // n_pairs) % 2
-            pair = (z // 2 + near_first[step % n_pairs]) % n_pairs
-            q = quarter_of(core, from_y)
+        def z_wait(q, step, of):
+            k = step * n_z + (z + n_z - of) % n_z
+
+            @pl.when(k > 0)
+            def _():
+                z_copy(it, k, q, of).wait()
+
+        for step in range(n_pairs):
+            pair = (z // 2 + near_first[step]) % n_pairs
             for e in range(2):
-                of = pair * 2 + e
-                k = (step // n_pairs) * n_z + (z + n_z - of) % n_z
-
-                @pl.when(k > 0)
-                def _():
-                    z_copy(it, k, q, of).wait()
-
-            if step % n_pairs == n_pairs - 1:
-                c_copy(it, step // n_pairs, q).start()
+                z_wait(q, 0, pair * 2 + e)
+            if step == n_pairs - 1:
+                c_copy(it, 0, q).start()
 
             @pl.when(it < ITERS - 1)
             def _():
@@ -394,13 +403,16 @@
                 else:
                     t_sum[...] += part
 
+        q_next = quarter_of(core, y + 1)
+        for of in range(n_z):
+            z_wait(q_next, 1, of)
+        c_copy(it, 1, q_next).start()
+
         @pl.when(it < ITERS - 1)
         def _():
-            of = quarter_of(core + 1, y)
-            c_copy(it, 0, of).wait()
-            t_sum[...] += dot_nt(source_block(of), tile[:, at(of, quarter)])
-            of = quarter_of(core + 1, y + 1)
-            c_copy(it, 1, of).wait()
+            t_sum[...] += dot_nt(source_block(q_next), tile[:, at(q_next, quarter)])
+            for i in range(2):
+                c_copy(it, i, quarter_of(core + 1, y + i)).wait()
 
             total = jnp.zeros((8, LANES), f32)
             for i in range(n_chunks):
@@ -410,13 +422,13 @@
                 total = total + now
             for k in range(n_ves):
                 t_send[k, :, chunk:] = total
+            there = (core + 1) % 2
+            pair_block = jnp.concatenate([source_block(there * 2), source_block(there * 2 + 1)], axis=1)
 
             def last(i, carry):
                 k = n_ves - 1 - i
                 rows = at(ves_at(k), chunk)
-                t_send[k, :, :chunk] = t_sum[:, rows] + dot_nt(
-                    source_block(of), tile[rows, at(of, quarter)]
-                )
+                t_send[k, :, :chunk] = t_sum[:, rows] + dot_nt(pair_block, tile[rows, at(there, 2 * quarter)])
 
                 @pl.when(k > 0)
                 def _():
@@ -424,7 +436,8 @@
 
                 return carry
 
-            lax.fori_loop(0, n_ves, last, 0)
+            for i in range(n_ves):
+                last(i, 0)
 
         @pl.when(it == ITERS - 1)
         def _():

time: 116 us -> 111 us (0.957)
  Pallas kernels: 115 us -> 110 us
    pallas_call x1, Pallas kernels: 113 us -> 108 us  [body(): pl.pallas_call(functools.partial(kernel, n_ves, n_z, pts, segs), out_shap...]
where the time goes in v3:
time: 111 us
  Pallas kernels  110 us (99%)
    pallas_call x1, Pallas kernels, body(): pl.pallas_call(functools.partial(kernel, n_ves, n_z, pts, segs), out_shap...  108 us

profile of v3, /device:TPU:1, one launch (start us, length us, event | category | flops | bytes accessed | tf_op | source)
XLA Modules:
  0.0 110.8 jit_solution(6780046250428460091)
XLA Ops:
  0.6 108.4 %exchange.1 = (f32[8,4096]{1,0:T(8,128)}, f32[8,4096]{1,0:T(8,128)}, f32[8,4096]{1,0:T(8,128)}) custom-call(f32[3,4096]{1,0:T(4,128)} %point_ref.1, s32[1,4096]{1,0:T(1,128)} %bitcast.5, f32[3,4096]{1,0:T(4,128)} %seg_ref.1, f32[1,4096]{1,0:T(1,128)} %bitcast.6, f32[1,4096]{1,0:T(1,128)} %bitcast.7, f32[1,4096]{1,0:T(1,128)} %bitcast.8, s32[1,4096]{1,0:T(1,128)} %bitcast.9, ...), custom_call_target="tpu_custom_call" | custom-call | tf_op jit(solution)/shard_map/exchange/pallas_call | solution.py:489
  109.0 1.8 %hand_over.1 = (f32[8,4096]{1,0:T(8,128)}, f32[8,4096]{1,0:T(8,128)}, f32[8,4096]{1,0:T(8,128)}) custom-call(f32[8,4096]{1,0:T(8,128)} %get-tuple-element.6.a, f32[8,4096]{1,0:T(8,128)} %get-tuple-element.7.b, f32[8,4096]{1,0:T(8,128)} %get-tuple-element.8.c), custom_call_target="tpu_custom_call" | custom-call | tf_op jit(solution)/shard_map/hand_over/pallas_call | solution.py:555

commit v4 on v3

--- a/solution.py
+++ b/solution.py
@@ -267,7 +267,7 @@
             summed = summed + t_recv[it, k - 1]
         level[it, v] = base[:, :1] + summed[:, :chunk] / (diff * total_segs)
 
-        for k in range(n_ves - 1, 0, -1):
+        for k in sorted(range(1, n_ves), key=lambda k: k // n_x * 2 + min(k % n_x, n_x - k % n_x)):
             l_copy(it, k, v).start()
         o_copy(it).start()
         sink_sum[...] = jnp.zeros_like(sink_sum)

time: 111 us -> 111 us (level)
  no operation moved by 1% of the time
where the time goes in v4:
time: 111 us; the launch traced here: 110 us
  Pallas kernels  110 us (99%)
    pallas_call x1, Pallas kernels, body(): pl.pallas_call(functools.partial(kernel, n_ves, n_z, pts, segs), out_shap...  108 us

profile of v4, /device:TPU:1, one launch (start us, length us, event | category | flops | bytes accessed | tf_op | source)
XLA Modules:
  0.0 110.4 jit_solution(12884416128485915837)
XLA Ops:
  0.6 108.0 %exchange.1 = (f32[8,4096]{1,0:T(8,128)}, f32[8,4096]{1,0:T(8,128)}, f32[8,4096]{1,0:T(8,128)}) custom-call(f32[3,4096]{1,0:T(4,128)} %point_ref.1, s32[1,4096]{1,0:T(1,128)} %bitcast.5, f32[3,4096]{1,0:T(4,128)} %seg_ref.1, f32[1,4096]{1,0:T(1,128)} %bitcast.6, f32[1,4096]{1,0:T(1,128)} %bitcast.7, f32[1,4096]{1,0:T(1,128)} %bitcast.8, s32[1,4096]{1,0:T(1,128)} %bitcast.9, ...), custom_call_target="tpu_custom_call" | custom-call | tf_op jit(solution)/shard_map/exchange/pallas_call | solution.py:489
  108.6 1.8 %hand_over.1 = (f32[8,4096]{1,0:T(8,128)}, f32[8,4096]{1,0:T(8,128)}, f32[8,4096]{1,0:T(8,128)}) custom-call(f32[8,4096]{1,0:T(8,128)} %get-tuple-element.6.a, f32[8,4096]{1,0:T(8,128)} %get-tuple-element.7.b, f32[8,4096]{1,0:T(8,128)} %get-tuple-element.8.c), custom_call_target="tpu_custom_call" | custom-call | tf_op jit(solution)/shard_map/hand_over/pallas_call | solution.py:555
